TPU v7x, 256 devices: a whole 4x4x8 slice. The times are simulated.
256 devices in a mesh: attn: 16 (over z, y_lo), exp: 16 (over x, y_hi, core).
Axes of the slice: x: 4, y: 4 (y_hi: 2, y_lo: 2; y = y_hi * 2 + y_lo), z: 8, core: 2. Of those that a mesh axis runs over, the one named last changes fastest.
Arguments:
- hidden_rows: bfloat16 [4096, 2880], P('attn'), may hold values from -6 to 6
- attention_gain: float32 [2880], replicated, may hold values from 0.1 to 1.9
- input_weight: bfloat16 [2880, 2560], P(None, 'exp'), may hold values from -0.109375 to 0.109375
- cache_keys: bfloat16 [4096, 128, 256], P(('attn', 'exp')), may hold values from -128 to 128
- cache_values: bfloat16 [4096, 128, 256], P(('attn', 'exp')), may hold values from -6 to 6
- context_length: int32 [4096], P(('attn', 'exp')), may hold values from 1 to 255
- sink_logits: float32 [32], replicated, may hold values from 2 to 7
- out_weight: bfloat16 [2048, 2880], P('exp'), may hold values from -0.125 to 0.125
- expert_gain: float32 [2880], replicated, may hold values from 0.1 to 1.9
- expert_index: int32 [4096, 4], P(('attn', 'exp')), may hold values from 0 to 63, all different within a row; in each aligned block of 16 rows (0 to 15, 16 to 31, ...) at most 2 rows name the same one
- expert_share: float32 [4096, 4], P(('attn', 'exp')), may hold values from 0.05 to 1
- gate_weight: bfloat16 [92160, 2880], P(('attn', 'exp')), may hold values from -0.109375 to 0.109375
- up_weight: bfloat16 [92160, 2880], P(('attn', 'exp')), may hold values from -0.109375 to 0.109375
- down_weight: bfloat16 [92160, 2880], P(('attn', 'exp')), may hold values from -0.15625 to 0.15625
Outputs:
- layer_out: bfloat16 [4096, 2880], P(('attn', 'exp'))
Inputs may be any that keep to these rules, and one draw needn't show every extreme that they name: `expert_index`: A row names 4 different experts. In each aligned block of 16 rows no expert is named more than 2 times, a bound that some block reaches.
All inputs are finite; a program needn't handle non-finite values.
Results may differ from a plain program's by a relative error of at most 0.019.
Values may be sent and summed in bfloat16 or wider, within the bound.
A program may use at most 64 MiB of HBM per device.

v0:
```python
import jax
import jax.numpy as jnp
from jax import lax
from jax.sharding import PartitionSpec as P

HEAD = 64
QHEADS = 32
KVHEADS = 4
TOPK = 4
CAP = 2
EXP_ATTN = 4
TOK_DEV = 16


def normed(values, gain_vec):
    widened = values.astype(jnp.float32)
    return (
        widened * lax.rsqrt(jnp.mean(widened * widened, axis=-1, keepdims=True) + 1e-05) * gain_vec
    )


def rotated(blocks, positions):
    half_dim = blocks.shape[-1] // 2
    frequency = 150000.0 ** (-jnp.arange(half_dim, dtype=jnp.float32) / half_dim)
    angles = positions.astype(jnp.float32)[:, None, None] * frequency
    cosine = jnp.cos(angles)
    sine_part = jnp.sin(angles)
    first_half = blocks[..., :half_dim]
    second_half = blocks[..., half_dim:]
    return jnp.concatenate(
        [
            first_half * cosine - second_half * sine_part,
            second_half * cosine + first_half * sine_part,
        ],
        axis=-1,
    )


def expert_part(rows_in, gate_rows, up_rows, down_rows):
    flat_rows = rows_in.reshape(-1, rows_in.shape[-1])
    contract = (((1,), (1,)), ((), ()))
    gate_out = lax.dot_general(flat_rows, gate_rows, contract, preferred_element_type=jnp.float32)
    up_out = lax.dot_general(flat_rows, up_rows, contract, preferred_element_type=jnp.float32)
    active = (jax.nn.silu(gate_out) * up_out).astype(jnp.bfloat16)
    return (
        jnp.dot(active, down_rows, preferred_element_type=jnp.float32)
        .astype(jnp.bfloat16)
        .reshape(rows_in.shape)
    )


def per_device(
    hidden_rows,
    attention_gain,
    input_weight,
    cache_keys,
    cache_values,
    context_length,
    sink_logits,
    out_weight,
    expert_gain,
    expert_index,
    expert_share,
    gate_weight,
    up_weight,
    down_weight,
):
    exp_count = lax.axis_size("exp")
    attn_count = lax.axis_size("attn")
    exp_index = lax.axis_index("exp")
    group_size = QHEADS // KVHEADS
    query_width = QHEADS * HEAD
    key_width = KVHEADS * HEAD
    score_scale = HEAD ** (-0.5)
    window_len = cache_keys.shape[1]
    normed_in = normed(hidden_rows, attention_gain).astype(jnp.bfloat16)
    projected = jnp.dot(normed_in, input_weight, preferred_element_type=jnp.float32).astype(
        jnp.bfloat16
    )
    own_proj = lax.all_to_all(projected, "exp", split_axis=0, concat_axis=1, tiled=True).astype(
        jnp.float32
    )
    row_count = own_proj.shape[0]
    queries = rotated(own_proj[:, :query_width].reshape(row_count, QHEADS, HEAD), context_length)
    new_keys = rotated(
        own_proj[:, query_width : query_width + key_width].reshape(row_count, KVHEADS, HEAD),
        context_length,
    )
    new_values = own_proj[:, query_width + key_width :].reshape(row_count, KVHEADS, HEAD)
    query_heads = queries.reshape(row_count, KVHEADS, group_size, HEAD)
    key_heads = cache_keys.astype(jnp.float32).reshape(row_count, window_len, KVHEADS, HEAD)
    value_heads = cache_values.astype(jnp.float32).reshape(row_count, window_len, KVHEADS, HEAD)
    scores = jnp.einsum("rkgd,rwkd->rkgw", query_heads, key_heads) * score_scale
    slot_index = jnp.arange(window_len, dtype=jnp.int32)
    valid_mask = (slot_index[None, :] >= window_len - context_length[:, None])[:, None, None, :]
    own_score = jnp.einsum("rkgd,rkd->rkg", query_heads, new_keys) * score_scale
    sink_part = sink_logits.reshape(1, KVHEADS, group_size)
    highest = jnp.maximum(
        jnp.max(jnp.where(valid_mask, scores, -1e30), axis=-1), jnp.maximum(own_score, sink_part)
    )
    weights = jnp.where(valid_mask, jnp.exp(scores - highest[..., None]), 0.0)
    own_weight = jnp.exp(own_score - highest)
    denominator = jnp.sum(weights, axis=-1) + own_weight + jnp.exp(sink_part - highest)
    mixed_rows = (
        jnp.einsum("rkgw,rwkd->rkgd", weights, value_heads)
        + own_weight[..., None] * new_values[:, :, None, :]
    )
    attended_own = (
        (mixed_rows / denominator[..., None]).reshape(row_count, query_width).astype(jnp.bfloat16)
    )
    attended = lax.all_to_all(attended_own, "exp", split_axis=1, concat_axis=0, tiled=True)
    attention_out = lax.psum_scatter(
        jnp.dot(attended, out_weight, preferred_element_type=jnp.float32).astype(jnp.bfloat16),
        "exp",
        scatter_dimension=0,
        tiled=True,
    ).astype(jnp.float32)
    residual = (
        lax.dynamic_slice_in_dim(hidden_rows, exp_index * TOK_DEV, TOK_DEV, 0).astype(jnp.float32)
        + attention_out
    )
    expert_in = normed(residual, expert_gain).astype(jnp.bfloat16)
    quarters = exp_count // EXP_ATTN
    expert_total = EXP_ATTN * attn_count
    width = expert_in.shape[1]
    pair_ids = expert_index.reshape(-1)
    onehot = (pair_ids[:, None] == jnp.arange(expert_total, dtype=jnp.int32)[None, :]).astype(
        jnp.int32
    )
    earlier = jnp.cumsum(onehot, axis=0, dtype=jnp.int32) - onehot
    slot_of = jnp.sum(earlier * onehot, axis=1, dtype=jnp.int32)
    target = pair_ids * CAP + slot_of
    placing = jnp.any(
        jnp.arange(expert_total * CAP, dtype=jnp.int32)[:, None, None]
        == target.reshape(TOK_DEV, TOPK)[None],
        axis=-1,
    ).astype(jnp.bfloat16)
    outgoing = (
        jnp.dot(placing, expert_in, preferred_element_type=jnp.float32)
        .astype(jnp.bfloat16)
        .reshape(attn_count, EXP_ATTN, CAP, width)
    )
    spread_rows = jnp.repeat(outgoing, quarters, axis=1)
    arrived = lax.all_to_all(
        lax.all_to_all(spread_rows, "attn", split_axis=0, concat_axis=0, tiled=True),
        "exp",
        split_axis=1,
        concat_axis=1,
        tiled=True,
    )
    partial_value = expert_part(arrived, gate_weight, up_weight, down_weight)
    returned = lax.all_to_all(
        lax.all_to_all(partial_value, "attn", split_axis=0, concat_axis=0, tiled=True),
        "exp",
        split_axis=1,
        concat_axis=1,
        tiled=True,
    )
    summed = (
        returned.astype(jnp.float32)
        .reshape(attn_count, EXP_ATTN, quarters, CAP, width)
        .sum(axis=2)
        .astype(jnp.bfloat16)
    )
    results = lax.optimization_barrier(summed).reshape(expert_total * CAP, width)
    picked = jnp.take(results, target, axis=0).astype(jnp.float32)
    weighted = (picked * expert_share.reshape(-1)[:, None]).reshape(TOK_DEV, TOPK, width)
    return (residual + jnp.sum(weighted, axis=1)).astype(jnp.bfloat16)


def solution(mesh):
    return jax.shard_map(
        per_device,
        mesh=mesh,
        in_specs=(
            P("attn", None),
            P(),
            P(None, "exp"),
            P(("attn", "exp"), None, None),
            P(("attn", "exp"), None, None),
            P(("attn", "exp")),
            P(),
            P("exp", None),
            P(),
            P(("attn", "exp"), None),
            P(("attn", "exp"), None),
            P(("attn", "exp"), None),
            P(("attn", "exp"), None),
            P(("attn", "exp"), None),
        ),
        out_specs=P(("attn", "exp"), None),
        check_vma=False,
    )
```

profile of v0, /device:TPU:1, one launch (start us, length us, event | category | flops | bytes accessed | tf_op | source)
XLA Modules:
  0.0 426.9 jit_solution(316781920849408814)
XLA Ops:
  6.5 1.9 fusion
  8.5 2.4 fusion.10
  11.6 8.4 %all-to-all-start = ((bf16[16,16,160]{2,1,0:T(8,128)(2,1)}), bf16[16,16,160]{2,1,0:T(8,128)(2,1)S(1)}, u32[]{:S(2)}, u32[]{:S(2)}) async-start(bf16[16,16,160]{2,1,0:T(8,128)(2,1)} %bitcast), calls=%async_computation | async-start | bytes 262144 | tf_op jit(solution)/shard_map/all_to_all | solution.py:80
  22.1 2.3 copy.66
  24.3 3.4 all-to-all-done
  35.9 11.0 %all_to_all.49 = bf16[16,16,128]{2,0,1:T(8,128)(2,1)S(1)} all-to-all(bf16[16,16,128]{2,0,1:T(8,128)(2,1)S(1)} %copy.67), channel_id=1, replica_groups=mesh['attn'=16,'exp'=16] {'exp'}, dimensions={1} | all-to-all | bytes 131072 | tf_op jit(solution)/shard_map/all_to_all | solution.py:111
  46.9 2.9 convolution_convert_fusion.1
  52.2 69.9 %reduce-scatter.2.cloned.1.call-done = bf16[16,2880]{1,0:T(8,128)(2,1)} async-done(((bf16[256,2880]{1,0:T(8,128)(2,1)}), bf16[16,2880]{1,0:T(8,128)(2,1)}) %reduce-scatter.2.cloned.1.call-update) | async-done | bytes 92176 | tf_op jit(solution)/shard_map/reduce_scatter | solution.py:112
  125.7 2.1 reshape.213
  129.4 73.9 %all_to_all.50 = bf16[16,16,2,2880]{3,2,1,0:T(2,128)(2,1)S(1)} all-to-all(bf16[16,16,2,2880]{3,2,1,0:T(2,128)(2,1)S(1)} %bitcast.42), channel_id=1, replica_groups=mesh['attn'=16,'exp'=16] {'attn'}, dimensions={0} | all-to-all | bytes 5898240 | tf_op jit(solution)/shard_map/all_to_all | solution.py:145
  203.3 2.1 copy.72
  205.4 47.4 %all_to_all.51 = bf16[16,16,2,2880]{3,2,0,1:T(2,128)(2,1)S(1)} all-to-all(bf16[16,16,2,2880]{3,2,0,1:T(2,128)(2,1)S(1)} %copy.72), channel_id=1, replica_groups=mesh['attn'=16,'exp'=16] {'exp'}, dimensions={1} | all-to-all | bytes 5898240 | tf_op jit(solution)/shard_map/all_to_all | solution.py:144
  252.8 3.7 copy.73
  256.5 7.1 %reshape.215 = bf16[512,2880]{1,0:T(8,128)(2,1)} reshape(bf16[16,16,2,2880]{3,2,1,0:T(2,128)(2,1)} %copy.73) | data formatting | bytes 5898240 | tf_op jit(solution)/shard_map/reshape | solution.py:40
  263.7 3.8 fusion.36
  267.6 7.2 %convolution_convert_fusion = bf16[512,2880]{0,1:T(8,128)(2,1)} fusion(bf16[360,2880]{1,0:T(8,128)(2,1)S(1)} %copy-done, bf16[512,2880]{1,0:T(8,128)(2,1)} %reshape.215, bf16[360,2880]{1,0:T(8,128)(2,1)} %param.26, f32[512,360]{0,1:T(8,128)S(1)} %fusion.36), kind=kOutput, calls=%fused_computation.1 | convolution fusion | flops 2125946880 | bytes 10782720 | tf_op jit(solution)/shard_map/dot_general | solution.py:46
  274.7 4.6 %copy.74 = bf16[512,2880]{1,0:T(8,128)(2,1)} copy(bf16[512,2880]{0,1:T(8,128)(2,1)} %convolution_convert_fusion) | data formatting | bytes 5898240 | tf_op jit(solution)/shard_map/convert_element_type | solution.py:47
  279.3 6.9 %reshape.216 = bf16[16,16,2,2880]{3,2,1,0:T(2,128)(2,1)} reshape(bf16[512,2880]{1,0:T(8,128)(2,1)} %copy.74) | data formatting | bytes 5898240 | tf_op jit(solution)/shard_map/reshape | solution.py:48
  286.2 73.2 %all_to_all.52 = bf16[16,16,2,2880]{3,2,1,0:T(2,128)(2,1)S(1)} all-to-all(bf16[16,16,2,2880]{3,2,1,0:T(2,128)(2,1)} %reshape.216), channel_id=1, replica_groups=mesh['attn'=16,'exp'=16] {'attn'}, dimensions={0} | all-to-all | bytes 5898240 | tf_op jit(solution)/shard_map/all_to_all | solution.py:153
  359.4 3.7 copy.75
  363.1 7.1 %all-to-all-start.5 = ((bf16[16,16,2,2880]{3,2,0,1:T(2,128)(2,1)}), bf16[16,16,2,2880]{3,2,0,1:T(2,128)(2,1)}, u32[]{:S(2)}, u32[]{:S(2)}) async-start(bf16[16,16,2,2880]{3,2,0,1:T(2,128)(2,1)} %copy.75), calls=%async_computation.6 | async-start | bytes 6029312 | tf_op jit(solution)/shard_map/all_to_all | solution.py:152
  370.4 38.3 %all-to-all-done.5 = bf16[16,16,2,2880]{3,2,0,1:T(2,128)(2,1)} async-done(((bf16[16,16,2,2880]{3,2,0,1:T(2,128)(2,1)}), bf16[16,16,2,2880]{3,2,0,1:T(2,128)(2,1)}, u32[]{:S(2)}, u32[]{:S(2)}) %all-to-all-start.5) | async-done | bytes 2949152 | tf_op jit(solution)/shard_map/all_to_all | solution.py:152
  408.7 5.5 %bitcast_reduce_fusion = bf16[16,4,2,2880]{3,2,0,1:T(2,128)(2,1)S(1)} fusion(bf16[16,16,2,2880]{3,2,0,1:T(2,128)(2,1)} %all-to-all-done.5), kind=kLoop, calls=%fused_computation.6 | loop fusion | flops 1105920 | bytes 3686400 | tf_op jit(solution)/shard_map/reduce_sum | solution.py:162
  415.6 2.3 reshape.219
  (69 shorter events, 22.2 us)
Async XLA Ops:
  6.5 261.0 %copy-start = (bf16[360,2880]{1,0:T(8,128)(2,1)S(1)}, bf16[360,2880]{1,0:T(8,128)(2,1)}, u32[]{:S(2)}) copy-start(bf16[360,2880]{1,0:T(8,128)(2,1)} %param.27) | copy-start | bytes 6220804
  6.5 13.6 %copy-start.6 = (s32[16]{0:T(128)S(1)}, s32[16]{0:T(128)}, u32[]{:S(2)}) copy-start(s32[16]{0:T(128)} %param.19) | copy-start | bytes 196
  8.5 13.5 %copy-start.5 = (f32[32]{0:T(128)S(1)}, f32[32]{0:T(128)}, u32[]{:S(2)}) copy-start(f32[32]{0:T(128)} %param.20) | copy-start | bytes 388
  11.6 16.1 %all-to-all-start = ((bf16[16,16,160]{2,1,0:T(8,128)(2,1)}), bf16[16,16,160]{2,1,0:T(8,128)(2,1)S(1)}, u32[]{:S(2)}, u32[]{:S(2)}) async-start(bf16[16,16,160]{2,1,0:T(8,128)(2,1)} %bitcast), calls=%async_computation | async-start | bytes 262144 | tf_op jit(solution)/shard_map/all_to_all | solution.py:80
  20.1 102.1 %reduce-scatter.2.cloned.1.call-start = ((), (), s32[]{:S(2)}) async-start(), calls=%async_computation.7 | async-start | bytes 1601536 | tf_op jit(solution)/shard_map/reduce_scatter | solution.py:112
  46.8 4.6 %copy-start.3 = (s32[16,4]{0,1:T(4,128)S(1)}, s32[16,4]{0,1:T(4,128)}, u32[]{:S(2)}) copy-start(s32[16,4]{0,1:T(4,128)} %param.23) | copy-start | bytes 772
  46.9 76.3 %copy-start.2 = (f32[2880]{0:T(1024)S(1)}, f32[2880]{0:T(1024)}, u32[]{:S(2)}) copy-start(f32[2880]{0:T(1024)} %param.22) | copy-start | bytes 34564
  363.1 7.2 %copy-start.4 = (f32[16,4]{0,1:T(4,128)S(1)}, f32[16,4]{0,1:T(4,128)}, u32[]{:S(2)}) copy-start(f32[16,4]{0,1:T(4,128)} %param.24) | copy-start | bytes 772
  363.1 45.6 %all-to-all-start.5 = ((bf16[16,16,2,2880]{3,2,0,1:T(2,128)(2,1)}), bf16[16,16,2,2880]{3,2,0,1:T(2,128)(2,1)}, u32[]{:S(2)}, u32[]{:S(2)}) async-start(bf16[16,16,2,2880]{3,2,0,1:T(2,128)(2,1)} %copy.75), calls=%async_computation.6 | async-start | bytes 6029312 | tf_op jit(solution)/shard_map/all_to_all | solution.py:152
  415.6 3.8 copy-start.1
Sparse Core Ops, SparseCore 0:
  49.9 72.2 reduce-scatter.1
where the time goes:
time: 430 us; the launch traced here: 427 us
  blocking collectives  206 us (48%)
  waiting for transfers between devices  112 us (26%)
  local copies, waits for them, and re-layouts  49 us (11%)
  matrix products  20.4 us (5%)
  starting transfers between devices  15.6 us (4%)
  between operations  13.7 us (3%)
  other arithmetic  11.2 us (3%)
    all_to_all x1, blocking collectives, per_device(): lax.all_to_all(spread_rows, 'attn', split_axis=0, concat_axis=0, tiled=True)  73.9 us
    all_to_all x1, blocking collectives, per_device(): lax.all_to_all(partial_value, 'attn', split_axis=0, concat_axis=0, tiled=...  73.2 us
    reduce_scatter x1, waiting for transfers between devices, per_device(): lax.psum_scatter(jnp.dot(attended, out_weight, preferred_element_type=jnp...  69.9 us
    all_to_all x1, blocking collectives, per_device(): lax.all_to_all(lax.all_to_all(spread_rows, 'attn', split_axis=0, concat_a...  47.4 us
    all_to_all x1, waiting for transfers between devices, per_device(): lax.all_to_all(lax.all_to_all(partial_value, 'attn', split_axis=0, concat...  38.3 us
    all_to_all x1, blocking collectives, per_device(): lax.all_to_all(attended_own, 'exp', split_axis=1, concat_axis=0, tiled=True)  11 us
  transfers between devices with their start and end apart: 3, of which 3 were waited for; matrix products, arithmetic and copies ran while one was open for 2% of the time, Pallas kernels for 0%

commit v1 on v0

v1 whole, which is shorter than its diff:
```python
import jax
import jax.numpy as jnp
from jax import lax
from jax.experimental import pallas as pl
from jax.experimental.pallas import tpu as pltpu
from jax.sharding import PartitionSpec as P

HEAD = 64
QHEADS = 32
KVHEADS = 4
TOK_DEV = 16


def normed(values, gain_vec):
    widened = values.astype(jnp.float32)
    return (
        widened * lax.rsqrt(jnp.mean(widened * widened, axis=-1, keepdims=True) + 1e-05) * gain_vec
    )


def rotated(blocks, positions):
    half_dim = blocks.shape[-1] // 2
    frequency = 150000.0 ** (-jnp.arange(half_dim, dtype=jnp.float32) / half_dim)
    angles = positions.astype(jnp.float32)[:, None, None] * frequency
    cosine = jnp.cos(angles)
    sine_part = jnp.sin(angles)
    first_half = blocks[..., :half_dim]
    second_half = blocks[..., half_dim:]
    return jnp.concatenate(
        [
            first_half * cosine - second_half * sine_part,
            second_half * cosine + first_half * sine_part,
        ],
        axis=-1,
    )


D = 2880
FFQ = 360
CHUNKS = ((0, 768), (768, 768), (1536, 768), (2304, 576))
NC = len(CHUNKS)
BF = jnp.bfloat16
F32 = jnp.float32
MESH = pl.DeviceIdType.MESH
NT = (((1,), (1,)), ((), ()))


def place():
    attn = lax.axis_index("attn")
    exp = lax.axis_index("exp")
    return dict(
        attn=attn,
        exp=exp,
        z=lax.div(attn, 2),
        y_lo=lax.rem(attn, 2),
        x=lax.div(exp, 4),
        y_hi=lax.rem(lax.div(exp, 2), 2),
        core=lax.rem(exp, 2),
    )


def z_peer(me, d):
    other = lax.rem(me["z"] + d, 8)
    return other, (other * 2 + me["y_lo"], me["exp"])


def plane_peer(me, d):
    other = lax.rem(me["q"] + d, 16)
    y_hi, y_lo, x = lax.div(other, 8), lax.rem(lax.div(other, 4), 2), lax.rem(other, 4)
    return other, (me["z"] * 2 + y_lo, (x * 2 + y_hi) * 2 + me["core"])


def group_peer(me, d):
    other = lax.rem(me["g"] + d, 8)
    return other, (me["attn"], other * 2 + me["core"])


def remote(src, dst, send_sem, recv_sem, device):
    return pltpu.make_async_remote_copy(
        src_ref=src,
        dst_ref=dst,
        send_sem=send_sem,
        recv_sem=recv_sem,
        device_id=device,
        device_id_type=MESH,
    )


def wait_bytes(ref, sem):
    pltpu.make_async_copy(ref, ref, sem).wait()


def spread(count, peer, me, src, dst, own, send_sem, recv_sem):
    @pl.loop(1, count)
    def _(d):
        other, device = peer(me, d)
        remote(src.at[other], dst.at[own], send_sem, recv_sem, device).start()


def layer_tail(
    att,
    w_out,
    hidden,
    gain,
    index,
    share,
    gate_hbm,
    up_hbm,
    down_hbm,
    out,
    *scratch,
):
    s = dict(zip(SCRATCH_NAMES, scratch))
    part = {
        name: [s[f"{name}{c}"] for c in range(NC)] for name in CHUNKED
    }
    me = place()
    me["q"] = me["y_hi"] * 8 + me["y_lo"] * 4 + me["x"]
    me["g"] = me["x"] * 2 + me["y_hi"]
    core, partner = me["core"], (me["attn"], me["exp"] + 1 - 2 * me["core"])

    loads = [
        pltpu.make_async_copy(gate_hbm, s["gate"], s["load_sem"].at[0]),
        pltpu.make_async_copy(up_hbm, s["up"], s["load_sem"].at[1]),
        pltpu.make_async_copy(down_hbm, s["down"], s["load_sem"].at[2]),
    ]
    for load in loads:
        load.start()

    barrier = pltpu.get_barrier_semaphore()

    @pl.loop(1, 8)
    def _(d):
        pl.semaphore_signal(barrier, inc=1, device_id=z_peer(me, d)[1], device_id_type=MESH)

    @pl.loop(1, 16)
    def _(d):
        pl.semaphore_signal(barrier, inc=1, device_id=plane_peer(me, d)[1], device_id_type=MESH)

    pl.semaphore_signal(barrier, inc=1, device_id=partner, device_id_type=MESH)
    pl.semaphore_wait(barrier, 23)

    core_copies = []
    att_mine = att[:, pl.ds(core, 1)].reshape(128, 128)
    att_other = att[:, pl.ds(1 - core, 1)].reshape(128, 128)
    for c, (c0, width) in enumerate(CHUNKS):
        columns = w_out[:, c0 : c0 + width]
        part["rcs"][c][...] = jnp.dot(att_other, columns, preferred_element_type=F32).astype(BF)
        copy = remote(
            part["rcs"][c], part["rcr"][c], s["rc_send"].at[c], s["rc_recv"].at[c], partner
        )
        copy.start()
        core_copies.append(copy)
        part["rmine"][c][...] = jnp.dot(att_mine, columns, preferred_element_type=F32)
    for c, (c0, width) in enumerate(CHUNKS):
        core_copies[c].wait_recv()
        total = part["rmine"][c][...] + part["rcr"][c][...].astype(F32)
        part["rsum"][c][...] = total.astype(BF).reshape(8, 16, width)
        spread(
            8, group_peer, me, part["rsum"][c], part["rrec"][c], me["g"],
            s["rs_send"].at[c], s["rs_recv"].at[c],
        )
        part["rrec"][c][me["g"]] = part["rsum"][c][me["g"]]

    slot_lane = lax.broadcasted_iota(jnp.int32, (16, 128), 1)
    expert_lane = lax.div(slot_lane, 2)
    named = jnp.zeros((16, 128), F32)
    weight = jnp.zeros((16, 128), F32)
    for k in range(4):
        hit = index[:, k : k + 1] == expert_lane
        named = named + jnp.where(hit, 1.0, 0.0)
        weight = weight + jnp.where(hit, share[:, k : k + 1], 0.0)
    row = lax.broadcasted_iota(jnp.int32, (16, 16), 0)
    column = lax.broadcasted_iota(jnp.int32, (16, 16), 1)
    before = jnp.where(column < row, 1.0, 0.0).astype(BF)
    earlier = jnp.dot(before, named.astype(BF), preferred_element_type=F32)
    taken = jnp.where(earlier == lax.rem(slot_lane, 2).astype(F32), named, 0.0)
    weight = weight * taken
    weight_hi = weight.astype(BF)
    weight_lo = (weight - weight_hi.astype(F32)).astype(BF)
    wide_row = lax.broadcasted_iota(jnp.int32, (128, 128), 0)
    wide_column = lax.broadcasted_iota(jnp.int32, (128, 128), 1)
    identity = jnp.where(wide_row == wide_column, 1.0, 0.0).astype(BF)
    placing = lax.dot_general(identity, taken.astype(BF), NT, preferred_element_type=F32).astype(BF)
    by_expert = lax.rem(lax.div(wide_row, 2), 8) * 16 + lax.div(wide_row, 16) * 2 + lax.rem(wide_row, 2)
    to_expert = jnp.where(by_expert == wide_column, 1.0, 0.0).astype(BF)

    square_sum = jnp.zeros((16, 1), F32)
    for c, (c0, width) in enumerate(CHUNKS):
        wait_bytes(part["rrec"][c].at[0:7], s["rs_recv"].at[c])
        residual = hidden[:, c0 : c0 + width].astype(F32) + jnp.sum(
            part["rrec"][c][...].astype(F32), axis=0
        )
        s["residual"][:, c0 : c0 + width] = residual
        square_sum = square_sum + jnp.sum(residual * residual, axis=1, keepdims=True)
    scale = lax.rsqrt(square_sum / D + 1e-05)

    for c, (c0, width) in enumerate(CHUNKS):
        expert_in = (
            s["residual"][:, c0 : c0 + width] * scale * gain[:, c0 : c0 + width]
        ).astype(BF)
        placed = jnp.dot(placing, expert_in, preferred_element_type=F32).astype(BF)
        part["zs"][c][...] = placed.reshape(8, 16, width)
        spread(
            8, z_peer, me, part["zs"][c], part["zr"][c], me["z"],
            s["z_send"].at[c], s["z_recv"].at[c],
        )
        part["zr"][c][me["z"]] = part["zs"][c][me["z"]]

    def plane_out(c):
        width = CHUNKS[c][1]
        wait_bytes(part["zr"][c].at[0:7], s["z_recv"].at[c])
        rows = part["zr"][c][...].reshape(128, width)
        part["ps"][c][...] = (
            jnp.dot(to_expert, rows, preferred_element_type=F32).astype(BF).reshape(8, 16, width)
        )

        @pl.loop(1, 16)
        def _(d):
            other, device = plane_peer(me, d)
            remote(
                part["ps"][c].at[lax.rem(other, 8)],
                part["xin"][c].at[core, me["q"]],
                s["p_send"].at[c],
                s["p_recv"].at[c],
                device,
            ).start()

        part["xin"][c][core, me["q"]] = part["ps"][c][lax.rem(me["q"], 8)]

    swap_copies = {}

    def swap_out(c):
        mine = part["xin"][c].at[core]
        wait_bytes(part["xin"][c].at[0, 0:15], s["p_recv"].at[c])
        swap_copies[c] = remote(mine, mine, s["x_send"].at[c], s["x_recv"].at[c], partner)
        swap_copies[c].start()

    def hidden_units(c):
        c0, width = CHUNKS[c]
        swap_copies[c].wait_recv()
        if c == 0:
            loads[0].wait()
            loads[1].wait()
        rows = part["xin"][c][...].reshape(512, width)
        for weights, total in (("gate", "gate_out"), ("up", "up_out")):
            product = lax.dot_general(
                rows, s[weights][:, c0 : c0 + width], NT, preferred_element_type=F32
            )
            if c == 0:
                s[total][...] = product
            else:
                s[total][...] += product

    for step in range(NC + 2):
        if step < NC:
            plane_out(step)
        if 0 <= step - 1 < NC:
            swap_out(step - 1)
        if 0 <= step - 2 < NC:
            hidden_units(step - 2)

    gate_out = s["gate_out"][...]
    s["active"][...] = (gate_out / (1.0 + jnp.exp(-gate_out)) * s["up_out"][...]).astype(BF)
    loads[2].wait()

    back_copies = []
    for c, (c0, width) in enumerate(CHUNKS):
        columns = s["down"][:, c0 : c0 + width]
        other_rows = s["active"][pl.ds(pl.multiple_of((1 - core) * 256, 256), 256), :]
        part["ycs"][c][...] = jnp.dot(other_rows, columns, preferred_element_type=F32).astype(BF)
        copy = remote(
            part["ycs"][c], part["ycr"][c], s["y_send"].at[c], s["y_recv"].at[c], partner
        )
        copy.start()
        back_copies.append(copy)
        my_rows = s["active"][pl.ds(pl.multiple_of(core * 256, 256), 256), :]
        part["ymine"][c][...] = jnp.dot(my_rows, columns, preferred_element_type=F32)

    def plane_back(c):
        width = CHUNKS[c][1]
        back_copies[c].wait_recv()
        total = part["ymine"][c][...] + part["ycr"][c][...].astype(F32)
        part["ysum"][c][...] = total.astype(BF).reshape(16, 16, width)
        spread(
            16, plane_peer, me, part["ysum"][c], part["pr"][c], me["q"],
            s["b_send"].at[c], s["b_recv"].at[c],
        )
        part["pr"][c][me["q"]] = part["ysum"][c][me["q"]]

    back_row = lax.broadcasted_iota(jnp.int32, (128, 256), 0)
    back_column = lax.broadcasted_iota(jnp.int32, (128, 256), 1)
    by_source = (
        lax.rem(lax.div(back_row, 2), 8) * 16 + lax.div(back_row, 16) * 2 + lax.rem(back_row, 2)
    )
    to_source = jnp.where(by_source == lax.rem(back_column, 128), 1.0, 0.0).astype(BF)

    def z_back(c):
        width = CHUNKS[c][1]
        wait_bytes(part["pr"][c].at[0:15], s["b_recv"].at[c])
        rows = part["pr"][c][...].reshape(256, width)
        part["vs"][c][...] = (
            jnp.dot(to_source, rows, preferred_element_type=F32).astype(BF).reshape(8, 16, width)
        )
        spread(
            8, z_peer, me, part["vs"][c], part["vr"][c], me["z"],
            s["v_send"].at[c], s["v_recv"].at[c],
        )
        part["vr"][c][me["z"]] = part["vs"][c][me["z"]]

    def finish(c):
        c0, width = CHUNKS[c]
        wait_bytes(part["vr"][c].at[0:7], s["v_recv"].at[c])
        rows = part["vr"][c][...].reshape(128, width)
        mixed = jnp.dot(weight_hi, rows, preferred_element_type=F32) + jnp.dot(
            weight_lo, rows, preferred_element_type=F32
        )
        out[:, c0 : c0 + width] = (s["residual"][:, c0 : c0 + width] + mixed).astype(BF)

    for step in range(NC + 2):
        if step < NC:
            plane_back(step)
        if 0 <= step - 1 < NC:
            z_back(step - 1)
        if 0 <= step - 2 < NC:
            finish(step - 2)

    for c in range(NC):
        core_copies[c].wait_send()
        swap_copies[c].wait_send()
        back_copies[c].wait_send()
        wait_bytes(part["rsum"][c].at[0:7], s["rs_send"].at[c])
        wait_bytes(part["zs"][c].at[0:7], s["z_send"].at[c])
        wait_bytes(part["xin"][c].at[0, 0:15], s["p_send"].at[c])
        wait_bytes(part["ysum"][c].at[0:15], s["b_send"].at[c])
        wait_bytes(part["vs"][c].at[0:7], s["v_send"].at[c])


CHUNKED = {
    "rcs": ((128,), BF),
    "rcr": ((128,), BF),
    "rmine": ((128,), F32),
    "rsum": ((8, 16), BF),
    "rrec": ((8, 16), BF),
    "zs": ((8, 16), BF),
    "zr": ((8, 16), BF),
    "ps": ((8, 16), BF),
    "xin": ((2, 16, 16), BF),
    "ycs": ((256,), BF),
    "ycr": ((256,), BF),
    "ymine": ((256,), F32),
    "ysum": ((16, 16), BF),
    "pr": ((16, 16), BF),
    "vs": ((8, 16), BF),
    "vr": ((8, 16), BF),
}
SCRATCH = {
    f"{name}{c}": pltpu.VMEM((*lead, CHUNKS[c][1]), dtype)
    for name, (lead, dtype) in CHUNKED.items()
    for c in range(NC)
}
SCRATCH["gate"] = pltpu.VMEM((FFQ, D), BF)
SCRATCH["up"] = pltpu.VMEM((FFQ, D), BF)
SCRATCH["down"] = pltpu.VMEM((FFQ, D), BF)
SCRATCH["residual"] = pltpu.VMEM((16, D), F32)
SCRATCH["gate_out"] = pltpu.VMEM((512, FFQ), F32)
SCRATCH["up_out"] = pltpu.VMEM((512, FFQ), F32)
SCRATCH["active"] = pltpu.VMEM((512, FFQ), BF)
SCRATCH["load_sem"] = pltpu.SemaphoreType.DMA((3,))
for way in ("rc", "rs", "z", "p", "x", "y", "b", "v"):
    SCRATCH[f"{way}_send"] = pltpu.SemaphoreType.DMA((NC,))
    SCRATCH[f"{way}_recv"] = pltpu.SemaphoreType.DMA((NC,))
SCRATCH_NAMES = tuple(SCRATCH)


def run_tail(att, w_out, hidden, gain, index, share, gate, up, down):
    vmem = pl.BlockSpec(memory_space=pltpu.VMEM)
    anywhere = pl.BlockSpec(memory_space=pl.ANY)
    return pl.pallas_call(
        layer_tail,
        out_shape=jax.ShapeDtypeStruct((16, D), BF),
        in_specs=[vmem] * 6 + [anywhere] * 3,
        out_specs=vmem,
        scratch_shapes=list(SCRATCH.values()),
        compiler_params=pltpu.CompilerParams(
            collective_id=0, has_side_effects=True, vmem_limit_bytes=58 * 1024 * 1024
        ),
        cost_estimate=pl.CostEstimate(
            flops=3_600_000_000, bytes_accessed=8_000_000, transcendentals=200_000
        ),
        name="layer_tail",
    )(att, w_out, hidden, gain, index, share, gate, up, down)


def per_device(
    hidden_rows,
    attention_gain,
    input_weight,
    cache_keys,
    cache_values,
    context_length,
    sink_logits,
    out_weight,
    expert_gain,
    expert_index,
    expert_share,
    gate_weight,
    up_weight,
    down_weight,
):
    exp_index = lax.axis_index("exp")
    group_size = QHEADS // KVHEADS
    query_width = QHEADS * HEAD
    key_width = KVHEADS * HEAD
    score_scale = HEAD ** (-0.5)
    window_len = cache_keys.shape[1]
    normed_in = normed(hidden_rows, attention_gain).astype(jnp.bfloat16)
    projected = jnp.dot(normed_in, input_weight, preferred_element_type=jnp.float32).astype(
        jnp.bfloat16
    )
    own_proj = lax.all_to_all(projected, "exp", split_axis=0, concat_axis=1, tiled=True).astype(
        jnp.float32
    )
    row_count = own_proj.shape[0]
    queries = rotated(own_proj[:, :query_width].reshape(row_count, QHEADS, HEAD), context_length)
    new_keys = rotated(
        own_proj[:, query_width : query_width + key_width].reshape(row_count, KVHEADS, HEAD),
        context_length,
    )
    new_values = own_proj[:, query_width + key_width :].reshape(row_count, KVHEADS, HEAD)
    query_heads = queries.reshape(row_count, KVHEADS, group_size, HEAD)
    key_heads = cache_keys.astype(jnp.float32).reshape(row_count, window_len, KVHEADS, HEAD)
    value_heads = cache_values.astype(jnp.float32).reshape(row_count, window_len, KVHEADS, HEAD)
    scores = jnp.einsum("rkgd,rwkd->rkgw", query_heads, key_heads) * score_scale
    slot_index = jnp.arange(window_len, dtype=jnp.int32)
    valid_mask = (slot_index[None, :] >= window_len - context_length[:, None])[:, None, None, :]
    own_score = jnp.einsum("rkgd,rkd->rkg", query_heads, new_keys) * score_scale
    sink_part = sink_logits.reshape(1, KVHEADS, group_size)
    highest = jnp.maximum(
        jnp.max(jnp.where(valid_mask, scores, -1e30), axis=-1), jnp.maximum(own_score, sink_part)
    )
    weights = jnp.where(valid_mask, jnp.exp(scores - highest[..., None]), 0.0)
    own_weight = jnp.exp(own_score - highest)
    denominator = jnp.sum(weights, axis=-1) + own_weight + jnp.exp(sink_part - highest)
    mixed_rows = (
        jnp.einsum("rkgw,rwkd->rkgd", weights, value_heads)
        + own_weight[..., None] * new_values[:, :, None, :]
    )
    attended_own = (
        (mixed_rows / denominator[..., None]).reshape(row_count, query_width).astype(jnp.bfloat16)
    )
    attended = lax.all_to_all(attended_own, "exp", split_axis=1, concat_axis=0, tiled=True)
    hidden_own = lax.dynamic_slice_in_dim(hidden_rows, exp_index * TOK_DEV, TOK_DEV, 0)
    return run_tail(
        attended.reshape(8, 2, TOK_DEV, 128),
        out_weight,
        hidden_own,
        expert_gain[None, :],
        expert_index,
        expert_share,
        gate_weight,
        up_weight,
        down_weight,
    )


def solution(mesh):
    return jax.shard_map(
        per_device,
        mesh=mesh,
        in_specs=(
            P("attn", None),
            P(),
            P(None, "exp"),
            P(("attn", "exp"), None, None),
            P(("attn", "exp"), None, None),
            P(("attn", "exp")),
            P(),
            P("exp", None),
            P(),
            P(("attn", "exp"), None),
            P(("attn", "exp"), None),
            P(("attn", "exp"), None),
            P(("attn", "exp"), None),
            P(("attn", "exp"), None),
        ),
        out_specs=P(("attn", "exp"), None),
        check_vma=False,
    )
```

time: 430 us -> 123 us (0.29)
  blocking collectives: 206 us -> 0 us
  waiting for transfers between devices: 112 us -> 6.43 us
  Pallas kernels: 0 us -> 82.7 us
  local copies, waits for them, and re-layouts: 49 us -> 12.7 us
  matrix products: 20.4 us -> 4.94 us
  between operations: 13.7 us -> 0.2 us
  other arithmetic: 11.2 us -> 2.77 us
    all_to_all x4 -> x0, blocking collectives: 206 us -> none  [the longest x1 73.9 us: per_device(): lax.all_to_all(spread_rows, 'attn', split_axis=0, concat_axis=0, tiled=True)]
    pallas_call x0 -> x1, Pallas kernels: none -> 82.7 us  [run_tail(): pl.pallas_call(layer_tail, out_shape=jax.ShapeDtypeStruct((16, D), BF), i...]
    reduce_scatter x1 -> x0, waiting for transfers between devices: 69.9 us -> none  [per_device(): lax.psum_scatter(jnp.dot(attended, out_weight, preferred_element_type=jnp...]
    all_to_all x1, waiting for transfers between devices: 38.3 us -> 1.99 us  [per_device(): lax.all_to_all(attended_own, 'exp', split_axis=1, concat_axis=0, tiled=True)]
    reshape x5 -> x0, local copies, waits for them, and re-layouts: 18.5 us -> none  [the longest x1 7.14 us: expert_part(): flat_rows = rows_in.reshape(-1, rows_in.shape[-1])]
    dot_general x4 -> x0, matrix products: 15.2 us -> none  [the longest x1 7.15 us: expert_part(): jnp.dot(active, down_rows, preferred_element_type=jnp.float32)]
    all_to_all x3 -> x0, local copies, waits for them, and re-layouts: 9.53 us -> none  [the longest x1 3.73 us: per_device(): lax.all_to_all(lax.all_to_all(spread_rows, 'attn', split_axis=0, concat_a...]
    reduce_sum x3 -> x0, other arithmetic: 6.3 us -> none  [the longest x1 5.49 us: per_device(): summed = returned.astype(jnp.float32).reshape(attn_count, EXP_ATTN, quart...]
  transfers between devices with their start and end apart: 3 -> 2, of which waited for: 3 -> 2; matrix products, arithmetic and copies ran while one was open for 2% -> 7% of each run, Pallas kernels for 0% -> 0%
where the time goes in v1:
time: 123 us; the launch traced here: 122 us
  Pallas kernels  82.7 us (67%)
  local copies, waits for them, and re-layouts  12.7 us (10%)
  starting transfers between devices  12.1 us (10%)
  waiting for transfers between devices  6.43 us (5%)
  matrix products  4.94 us (4%)
  other arithmetic  2.77 us (2%)
    pallas_call x1, Pallas kernels, run_tail(): pl.pallas_call(layer_tail, out_shape=jax.ShapeDtypeStruct((16, D), BF), i...  82.7 us
    unnamed x25, local copies, waits for them, and re-layouts  9.62 us
    all_to_all x1, starting transfers between devices, per_device(): lax.all_to_all(projected, 'exp', split_axis=0, concat_axis=1, tiled=True)  8.45 us
    all_to_all x1, waiting for transfers between devices, per_device(): lax.all_to_all(projected, 'exp', split_axis=0, concat_axis=1, tiled=True)  4.44 us
    all_to_all x1, starting transfers between devices, per_device(): lax.all_to_all(attended_own, 'exp', split_axis=1, concat_axis=0, tiled=True)  3.66 us
  transfers between devices with their start and end apart: 2, of which 2 were waited for; matrix products, arithmetic and copies ran while one was open for 7% of the time, Pallas kernels for 0%

profile of v1, /device:TPU:1, one launch (start us, length us, event | category | flops | bytes accessed | tf_op | source)
XLA Modules:
  0.0 121.9 jit_solution(1910221466521491832)
XLA Ops:
  0.0 1.9 %fusion = f32[256]{0:T(256)S(1)} fusion(bf16[256,2880]{0,1:T(8,128)(2,1)} %param.14), kind=kLoop, calls=%fused_computation.2 | loop fusion | flops 2211584 | bytes 1475584 | tf_op jit(solution)/shard_map/reduce_sum | solution.py:17
  1.9 2.2 %fusion.9 = bf16[256,160]{0,1:T(8,128)(2,1)S(1)} fusion(bf16[2880,160]{0,1:T(8,128)(2,1)S(1)} %copy-done, bf16[256,2880]{0,1:T(8,128)(2,1)} %param.14, f32[2880]{0:T(1024)} %param.15, f32[256]{0:T(256)S(1)} %add_rsqrt_fusion), kind=kOutput, calls=%fused_computation.12 | convolution fusion | flops 238919680 | bytes 2490624 | tf_op jit(solution)/shard_map/dot_general | solution.py:418
  4.1 0.7 copy.22
  4.8 8.4 %all-to-all-start = ((bf16[16,16,160]{2,1,0:T(8,128)(2,1)}), bf16[16,16,160]{2,1,0:T(8,128)(2,1)S(1)}, u32[]{:S(2)}, u32[]{:S(2)}) async-start(bf16[16,16,160]{2,1,0:T(8,128)(2,1)} %bitcast), calls=%async_computation | async-start | bytes 262144 | tf_op jit(solution)/shard_map/all_to_all | solution.py:421
  13.5 0.7 copy.24
  14.3 2.2 %copy.25 = bf16[16,128,256]{1,2,0:T(8,128)(2,1)} copy(bf16[16,128,256]{2,1,0:T(8,128)(2,1)} %param.18) | data formatting | bytes 2097152 | tf_op args[4]
  16.5 4.4 %all-to-all-done = bf16[16,16,160]{2,1,0:T(8,128)(2,1)S(1)} async-done(((bf16[16,16,160]{2,1,0:T(8,128)(2,1)}), bf16[16,16,160]{2,1,0:T(8,128)(2,1)S(1)}, u32[]{:S(2)}, u32[]{:S(2)}) %all-to-all-start) | async-done | bytes 81952 | tf_op jit(solution)/shard_map/all_to_all | solution.py:421
  21.0 0.2 copy.23
  21.9 0.3 fusion.16
  22.1 0.5 select_reduce_fusion
  22.7 0.3 fusion.12
  23.1 1.9 %fusion.8 = bf16[16,4,8,64]{3,2,1,0:T(8,128)(2,1)S(1)} fusion(bf16[16,128,4,64]{1,3,2,0:T(8,128)(2,1)} %bitcast.26, f32[16,4,8,128]{3,2,1,0:T(8,128)S(1)} %get-tuple-element.18, f32[16,4,8]{2,1,0:T(4,128)S(1)} %exponential_add_fusion, f32[16,4,64]{2,1,0:T(4,128)S(1)} %mul.158, f32[16,4,8]{2,1,0:T(4,128)S(1)} %get-tuple-element.5, ...), kind=kOutput, calls=%fused_computation.11 | convolution fusion | flops 8650752 | bytes 1400832 | tf_op jit(solution)/shard_map/rkgw,rwkd->rkgd/dot_general | solution.py:446
  25.2 0.7 copy.26
  25.9 3.7 %all-to-all-start.1 = ((bf16[16,16,128]{2,0,1:T(8,128)(2,1)}), bf16[16,16,128]{2,0,1:T(8,128)(2,1)S(1)}, u32[]{:S(2)}, u32[]{:S(2)}) async-start(bf16[16,16,128]{2,0,1:T(8,128)(2,1)} %copy.26), calls=%async_computation.1 | async-start | bytes 131072 | tf_op jit(solution)/shard_map/all_to_all | solution.py:452
  29.6 0.3 constant_dynamic-slice_fusion
  29.8 0.9 copy.33.hidden
  30.7 2.3 %copy.28.w_out = bf16[128,2880]{1,0:T(8,128)(2,1)} copy(bf16[128,2880]{0,1:T(8,128)(2,1)} %param.21) | data formatting | bytes 1474560 | tf_op args[7]
  33.0 0.6 broadcast_in_dim.36.gain
  33.6 0.7 copy.29.index
  34.3 0.7 copy.30.share
  35.0 2.0 %all-to-all-done.1 = bf16[16,16,128]{2,0,1:T(8,128)(2,1)S(1)} async-done(((bf16[16,16,128]{2,0,1:T(8,128)(2,1)}), bf16[16,16,128]{2,0,1:T(8,128)(2,1)S(1)}, u32[]{:S(2)}, u32[]{:S(2)}) %all-to-all-start.1) | async-done | bytes 65568 | tf_op jit(solution)/shard_map/all_to_all | solution.py:452
  37.0 0.6 copy-done.3
  37.6 82.7 %layer_tail.1 = bf16[16,2880]{1,0:T(8,128)(2,1)} custom-call(bf16[8,2,16,128]{3,2,1,0:T(8,128)(2,1)} %bitcast.30, bf16[128,2880]{1,0:T(8,128)(2,1)} %copy.28.w_out, bf16[16,2880]{1,0:T(8,128)(2,1)} %copy.33.hidden, f32[1,2880]{1,0:T(1,128)} %broadcast_in_dim.36.gain, s32[16,4]{1,0:T(8,128)} %copy.29.index, f32[16,4]{1,0:T(8,128)} %copy.30.share, ...), custom_call_target="tpu_custom_call" | custom-call | flops 3600000000 | bytes 8000000 | tf_op jit(solution)/shard_map/layer_tail/pallas_call | solution.py:379
  120.3 1.5 %copy.35 = bf16[16,2880]{1,0:T(8,128)(2,1)} copy(bf16[16,2880]{1,0:T(8,128)(2,1)} %layer_tail.1) | data formatting | bytes 184320
  (36 shorter events, 1.3 us)
Async XLA Ops:
  0.0 1.9 %copy-start = (bf16[2880,160]{0,1:T(8,128)(2,1)S(1)}, bf16[2880,160]{0,1:T(8,128)(2,1)}, u32[]{:S(2)}) copy-start(bf16[2880,160]{0,1:T(8,128)(2,1)} %param.16) | copy-start | bytes 2764804
  1.9 11.4 %copy-start.8 = (s32[16]{0:T(128)S(1)}, s32[16]{0:T(128)}, u32[]{:S(2)}) copy-start(s32[16]{0:T(128)} %param.19) | copy-start | bytes 196
  1.9 11.6 %copy-start.2 = (bf16[16,128,256]{2,1,0:T(8,128)(2,1)S(1)}, bf16[16,128,256]{2,1,0:T(8,128)(2,1)}, u32[]{:S(2)}) copy-start(bf16[16,128,256]{2,1,0:T(8,128)(2,1)} %param.17) | copy-start | bytes 3145732
  4.1 10.1 %copy-start.7 = (f32[32]{0:T(128)S(1)}, f32[32]{0:T(128)}, u32[]{:S(2)}) copy-start(f32[32]{0:T(128)} %param.20) | copy-start | bytes 388
  4.8 16.1 %all-to-all-start = ((bf16[16,16,160]{2,1,0:T(8,128)(2,1)}), bf16[16,16,160]{2,1,0:T(8,128)(2,1)S(1)}, u32[]{:S(2)}, u32[]{:S(2)}) async-start(bf16[16,16,160]{2,1,0:T(8,128)(2,1)} %bitcast), calls=%async_computation | async-start | bytes 262144 | tf_op jit(solution)/shard_map/all_to_all | solution.py:421
  22.7 6.9 %copy-start.1 = (bf16[256,2880]{0,1:T(8,128)(2,1)S(1)}, bf16[256,2880]{0,1:T(8,128)(2,1)}, u32[]{:S(2)}) copy-start(bf16[256,2880]{0,1:T(8,128)(2,1)} %param.14) | copy-start | bytes 4423684
  25.1 7.9 %copy-start.4 = (f32[2880]{0:T(1024)S(1)}, f32[2880]{0:T(1024)}, u32[]{:S(2)}) copy-start(f32[2880]{0:T(1024)} %param.22) | copy-start | bytes 34564
  25.1 8.5 %copy-start.5 = (s32[16,4]{0,1:T(4,128)S(1)}, s32[16,4]{0,1:T(4,128)}, u32[]{:S(2)}) copy-start(s32[16,4]{0,1:T(4,128)} %param.23) | copy-start | bytes 772
  25.1 9.2 %copy-start.6 = (f32[16,4]{0,1:T(4,128)S(1)}, f32[16,4]{0,1:T(4,128)}, u32[]{:S(2)}) copy-start(f32[16,4]{0,1:T(4,128)} %param.24) | copy-start | bytes 772
  25.9 11.1 %all-to-all-start.1 = ((bf16[16,16,128]{2,0,1:T(8,128)(2,1)}), bf16[16,16,128]{2,0,1:T(8,128)(2,1)S(1)}, u32[]{:S(2)}, u32[]{:S(2)}) async-start(bf16[16,16,128]{2,0,1:T(8,128)(2,1)} %copy.26), calls=%async_computation.1 | async-start | bytes 131072 | tf_op jit(solution)/shard_map/all_to_all | solution.py:452
  37.0 0.6 copy-start.3

commit v2 on v0

v2 whole, which is shorter than its diff:
```python
import math
from types import SimpleNamespace

import jax
import jax.numpy as jnp
from jax import lax
from jax.experimental import pallas as pl
from jax.experimental.pallas import tpu as pltpu
from jax.sharding import PartitionSpec as P

D = 2880
FFQ = 360
CHUNKS = ((0, 512), (512, 512), (1024, 512), (1536, 512), (2048, 512), (2560, 320))
NC = len(CHUNKS)
DISPATCH_TIMES = ((0, 1), (2.1, 1), (4.2, 1), (6.3, 1), (7.4, 1))
RETURN_TIMES = ((0, 1), (1.1, 1), (4.2, 1), (7.3, 1))
WIDTHS = tuple((width + 127) // 128 * 128 for _, width in CHUNKS) + (128,)
BF = jnp.bfloat16
F32 = jnp.float32
MESH = pl.DeviceIdType.MESH
NT = (((1,), (1,)), ((), ()))
PA, AA, RC, RS, Z, PLANE, SWAP, BC, BP, BZ = range(10)


class Place:
    def __init__(self):
        self.attn = lax.axis_index("attn")
        self.exp = lax.axis_index("exp")
        self.z = lax.div(self.attn, 2)
        self.y_lo = lax.rem(self.attn, 2)
        self.x = lax.div(self.exp, 4)
        self.y_hi = lax.rem(lax.div(self.exp, 2), 2)
        self.core = lax.rem(self.exp, 2)
        self.y = self.y_hi * 2 + self.y_lo
        self.group = lax.div(self.exp, 2)
        self.q = self.y_hi * 8 + self.y_lo * 4 + self.x
        self.partner = (self.attn, self.exp + 1 - 2 * self.core)

    def z_peer(self, d):
        other = lax.rem(self.z + d, 8)
        return other, (other * 2 + self.y_lo, self.exp)

    def plane_peer(self, d):
        other = lax.rem(self.q + d, 16)
        y_hi, y_lo, x = lax.div(other, 8), lax.rem(lax.div(other, 4), 2), lax.rem(other, 4)
        return other, (self.z * 2 + y_lo, (x * 2 + y_hi) * 2 + self.core)

    def exp_peer(self, d):
        other = lax.rem(self.exp + d, 16)
        return other, (self.attn, other)

    def group_peer(self, d):
        other = lax.rem(self.group + d, 8)
        return other, (self.attn, other * 2 + self.core)


def remote(src, dst, send_sem, recv_sem, device):
    return pltpu.make_async_remote_copy(
        src_ref=src,
        dst_ref=dst,
        send_sem=send_sem,
        recv_sem=recv_sem,
        device_id=device,
        device_id_type=MESH,
    )


def fill(ref, values):
    width = values.shape[-1]
    if width == ref.shape[-1]:
        ref[...] = values
    else:
        ref[..., 0:width] = values
        ref[..., width:] = jnp.zeros((*values.shape[:-1], ref.shape[-1] - width), values.dtype)


def wait_bytes(ref, sem):
    pltpu.make_async_copy(ref, ref, sem).wait()


def pipelined(count, stages, times):
    order = [
        (first + pitch * c, late, c, stage)
        for late, (stage, (first, pitch)) in enumerate(zip(stages, times))
        for c in range(count)
    ]
    for _, _, c, stage in sorted(order, key=lambda entry: entry[:3]):
        stage(c)


def layer(
    context,
    sinks,
    hidden_hbm,
    w_in_hbm,
    gain_in_hbm,
    keys_hbm,
    values_hbm,
    w_out_hbm,
    gain_hbm,
    index_hbm,
    share_hbm,
    gate_hbm,
    up_hbm,
    down_hbm,
    out,
    *scratch,
):
    s = SimpleNamespace(**dict(zip(SCRATCH, scratch)))
    rest = iter(scratch[len(SCRATCH) :])
    part = SimpleNamespace(
        **{name: [next(rest) for _ in range(n)] for name, (n, _, _) in CHUNKED.items()}
    )
    me = Place()
    core = me.core

    def send(way, c, src, dst, device):
        copy = remote(src, dst, s.send_sem.at[way, c], s.recv_sem.at[way, c], device)
        copy.start()
        return copy

    loads = SimpleNamespace()
    for number, (name, source) in enumerate(
        dict(
            hidden=hidden_hbm,
            w_in=w_in_hbm,
            gain_in=gain_in_hbm,
            keys=keys_hbm,
            values=values_hbm,
            w_out=w_out_hbm,
            gain=gain_hbm,
            index=index_hbm,
            share=share_hbm,
            gate=gate_hbm,
            up=up_hbm,
            down=down_hbm,
        ).items()
    ):
        load = pltpu.make_async_copy(source, getattr(s, name), s.load_sem.at[number])
        setattr(loads, name, load)
    loads.hidden.start()
    loads.w_in.start()
    loads.gain_in.start()
    loads.gain.start()
    loads.index.start()
    loads.share.start()

    barrier = pltpu.get_barrier_semaphore()

    def greet(device):
        pl.semaphore_signal(barrier, inc=1, device_id=device, device_id_type=MESH)

    @pl.loop(1, 8)
    def _(d):
        greet(me.z_peer(d)[1])

    @pl.loop(1, 16)
    def _(d):
        greet(me.plane_peer(d)[1])

    @pl.loop(0, 8)
    def _(g):
        greet((me.attn, g * 2 + 1 - core))

    loads.w_in.wait()
    loads.gain_in.wait()
    s.w_gain[...] = (s.w_in[...].astype(F32) * s.gain_in[...][None, :]).astype(BF)
    loads.hidden.wait()
    for load in (loads.keys, loads.values, loads.w_out, loads.gate, loads.up, loads.down):
        load.start()
    projected = jnp.dot(s.w_gain[...], s.hidden[...], preferred_element_type=F32)
    row_squares = jnp.zeros((8, 256), F32)
    for first in range(0, D, 96):
        piece = s.hidden[first : first + 96, :].astype(F32)
        row_squares = row_squares + jnp.sum((piece * piece).reshape(12, 8, 256), axis=0)
    row_scale = lax.rsqrt(jnp.sum(row_squares, axis=0, keepdims=True) / D + 1e-05)
    projected = (projected * row_scale).astype(BF)
    wide = (
        lax.broadcasted_iota(jnp.int32, (256, 256), 0),
        lax.broadcasted_iota(jnp.int32, (256, 256), 1),
    )
    identity = jnp.where(wide[0] == wide[1], 1.0, 0.0).astype(BF)
    by_row = lax.dot_general(identity, projected, NT, preferred_element_type=F32).astype(BF)
    fill(s.proj_out, by_row.reshape(16, 16, 160))
    lane = lax.broadcasted_iota(jnp.int32, (16, 128), 1)
    pair = lax.rem(lane, 32)
    row_of = lax.broadcasted_iota(jnp.int32, (16, 128), 0)
    position = jnp.zeros((16, 128), F32)
    for r in range(16):
        position = jnp.where(row_of == r, context[r].astype(F32), position)
    angle = position * jnp.exp(pair.astype(F32) * (-math.log(150000.0) / 32))
    sine = jnp.sin(angle)
    sine = jnp.where(lax.rem(lane, 64) < 32, -sine, sine)
    turn = jnp.where(lane < 64, jnp.cos(angle), sine)
    place_lane = lax.broadcasted_iota(jnp.int32, (1, 640), 1)
    entry = lax.rem(place_lane, 128)
    half = lax.rem(lax.div(entry, 32), 2)
    half = jnp.where(entry < 64, half, 1 - half)
    source = lax.div(place_lane, 128) * 64 + half * 32 + lax.rem(entry, 32)
    s.spreading[...] = jnp.where(
        lax.broadcasted_iota(jnp.int32, (320, 640), 0) == source, 1.0, 0.0
    ).astype(BF)
    head_row = lax.broadcasted_iota(jnp.int32, (32, 256), 0)
    head_lane = lax.broadcasted_iota(jnp.int32, (32, 256), 1)
    own_block = lax.div(head_lane, 64) == lax.div(head_row, 8)
    tail_row = lax.broadcasted_iota(jnp.int32, (8, 256), 0)
    tail_block = lax.div(lax.broadcasted_iota(jnp.int32, (8, 256), 1), 64)
    slot_number = lax.broadcasted_iota(jnp.int32, (32, 128), 1)
    parity = lax.div(slot_number, 64) == lax.rem(
        lax.broadcasted_iota(jnp.int32, (32, 128), 0), 2
    )
    sink_row = lax.broadcasted_iota(jnp.int32, (32, 1), 0)
    sink = jnp.zeros((32, 1), F32)
    for h in range(32):
        sink = jnp.where(sink_row == h, sinks[h], sink)

    loads.index.wait()
    loads.share.wait()
    loads.gain.wait()
    index, share = s.index, s.share
    slot = lax.broadcasted_iota(jnp.int32, (128, 16), 0)
    named = jnp.zeros((128, 16), F32)
    weight = jnp.zeros((128, 16), F32)
    for k in range(4):
        hit = index[k : k + 1, :] == lax.div(slot, 2)
        named = named + jnp.where(hit, 1.0, 0.0)
        weight = weight + jnp.where(hit, share[k : k + 1, :], 0.0)
    small_row = lax.broadcasted_iota(jnp.int32, (16, 16), 0)
    small_column = lax.broadcasted_iota(jnp.int32, (16, 16), 1)
    before = jnp.where(small_row < small_column, 1.0, 0.0).astype(BF)
    earlier = jnp.dot(named.astype(BF), before, preferred_element_type=F32)
    taken = jnp.where(earlier == lax.rem(slot, 2).astype(F32), named, 0.0)
    placing = taken.astype(BF)
    weight = weight * taken
    small_identity = jnp.where(small_row == small_column, 1.0, 0.0).astype(BF)

    def flipped(part_of):
        return lax.dot_general(small_identity, part_of, NT, preferred_element_type=F32).astype(BF)

    weight_hi = flipped(weight.astype(BF))
    weight_lo = flipped((weight - weight.astype(BF).astype(F32)).astype(BF))

    own_row = lax.broadcasted_iota(jnp.int32, (16, 256), 1) == (
        lax.broadcasted_iota(jnp.int32, (16, 256), 0) + me.exp * 16
    )
    own_row = jnp.where(own_row, 1.0, 0.0).astype(BF)
    for c0, width in CHUNKS:
        s.own_hidden[:, c0 : c0 + width] = lax.dot_general(
            own_row, s.hidden[c0 : c0 + width, :], NT, preferred_element_type=F32
        )

    by_source = lax.broadcasted_iota(jnp.int32, (1, 128), 1)
    by_source = (
        lax.div(lax.rem(by_source, 16), 2) * 16 + lax.div(by_source, 16) * 2 + lax.rem(by_source, 2)
    )
    wide_row = lax.broadcasted_iota(jnp.int32, (128, 128), 0)
    to_expert = jnp.where(by_source == wide_row, 1.0, 0.0).astype(BF)
    by_expert = lax.rem(lax.broadcasted_iota(jnp.int32, (1, 256), 1), 128)
    by_expert = (
        lax.div(lax.rem(by_expert, 16), 2) * 16 + lax.div(by_expert, 16) * 2 + lax.rem(by_expert, 2)
    )
    back_row = lax.broadcasted_iota(jnp.int32, (128, 256), 0)
    to_source = jnp.where(by_expert == back_row, 1.0, 0.0).astype(BF)

    pl.semaphore_wait(barrier, 30)

    @pl.loop(1, 16)
    def _(d):
        other, device = me.exp_peer(d)
        send(PA, 0, s.proj_out.at[other], s.proj_in.at[me.group, core], device)

    s.proj_in[me.group, core] = s.proj_out[me.exp]
    wait_bytes(s.proj_out.at[0:15], s.recv_sem.at[PA, 0])
    even = s.proj_in[:, 0].reshape(128, 256)[:, 0:160]
    odd = s.proj_in[:, 1].reshape(128, 256)[:, 0:160]
    laid = jnp.dot(even, s.spreading[0:160, :], preferred_element_type=F32) + jnp.dot(
        odd, s.spreading[160:320, :], preferred_element_type=F32
    )
    for t in range(5):
        plain = laid[:, t * 128 : (t + 1) * 128].reshape(8, 16, 128)
        turned = plain * turn[None]
        turned = turned + pltpu.roll(turned, 64, 2)
        for m in range(8):
            h = 5 * m + t
            block = turned[m]
            if h >= 36:
                block = jnp.where(lane < 64, plain[m], 0.0)
                block = block + pltpu.roll(block, 64, 1)
            s.heads[h * 16 : (h + 1) * 16, :] = block

    loads.keys.wait()
    loads.values.wait()
    for r in range(16):
        heads = s.heads[pl.ds(r, 40, stride=16), :]
        query = heads[0:32]
        query = jnp.where(own_block, jnp.concatenate([query, query], axis=1), 0.0)
        new = heads[32:40]
        new = jnp.concatenate([new, new], axis=1)
        new_key = jnp.sum(jnp.where(tail_block == tail_row, new, 0.0), axis=0, keepdims=True)
        new_value = jnp.sum(jnp.where(tail_block == tail_row - 4, new, 0.0), axis=0, keepdims=True)
        scores = (
            lax.dot_general(query.astype(BF), s.keys[r], NT, preferred_element_type=F32) * 0.125
        )
        own_score = jnp.sum(query * new_key, axis=1, keepdims=True) * 0.125
        valid = slot_number >= 128 - context[r]
        highest = jnp.maximum(
            jnp.max(jnp.where(valid, scores, -1e30), axis=1, keepdims=True),
            jnp.maximum(own_score, sink),
        )
        weights = jnp.where(valid, jnp.exp(scores - highest), 0.0)
        own_weight = jnp.exp(own_score - highest)
        denominator = (
            jnp.sum(weights, axis=1, keepdims=True) + own_weight + jnp.exp(sink - highest)
        )
        mixed = jnp.dot(weights.astype(BF), s.values[r], preferred_element_type=F32)
        mixed = (mixed + own_weight * new_value) / denominator
        mixed = jnp.where(own_block, mixed, 0.0)
        mixed = mixed[:, 0:128] + mixed[:, 128:256]
        mixed = mixed + pltpu.roll(mixed, 64, 1)
        s.mixed[pl.ds(r, 32, stride=16), :] = jnp.where(parity, mixed, 0.0)
    s.att_out[...] = jnp.sum(s.mixed[...].reshape(16, 2, 16, 128), axis=1).astype(BF)

    @pl.loop(1, 16)
    def _(d):
        other, device = me.exp_peer(d)
        send(AA, 0, s.att_out.at[other], s.att.at[me.group, core], device)

    s.att[me.group, core] = s.att_out[me.exp]

    wait_bytes(s.att_out.at[0:15], s.recv_sem.at[AA, 0])
    att = s.att
    loads.w_out.wait()

    core_copies = []
    att_mine = att[:, pl.ds(core, 1)].reshape(128, 128)
    att_other = att[:, pl.ds(1 - core, 1)].reshape(128, 128)
    for c, (c0, width) in enumerate(CHUNKS):
        shares = lax.dot_general(
            att_other, s.w_out[c0 : c0 + width, :], NT, preferred_element_type=F32
        )
        fill(part.rcs[c], shares.astype(BF))
        core_copies.append(send(RC, c, part.rcs[c], part.rcr[c], me.partner))
    for c, (c0, width) in enumerate(CHUNKS):
        shares = lax.dot_general(
            att_mine, s.w_out[c0 : c0 + width, :], NT, preferred_element_type=F32
        )
        fill(part.rmine[c], shares)

    squares = []
    swap_copies = {}

    def group_out(c):
        if c == NC:
            return
        width = WIDTHS[c]
        core_copies[c].wait_recv()
        total = part.rmine[c][...] + part.rcr[c][...].astype(F32)
        part.rsum[c][...] = total.astype(BF).reshape(8, 16, width)

        @pl.loop(1, 8)
        def _(d):
            other, device = me.group_peer(d)
            send(RS, c, part.rsum[c].at[other], part.rrec[c].at[me.group], device)

        part.rrec[c][me.group] = part.rsum[c][me.group]

    def z_out(c):
        width = WIDTHS[c]
        if c < NC:
            c0, width = CHUNKS[c]
            wait_bytes(part.rrec[c].at[0:7], s.recv_sem.at[RS, c])
            residual = s.own_hidden[:, c0 : c0 + width] + jnp.sum(
                part.rrec[c][:, :, 0:width].astype(F32), axis=0
            )
            s.residual[:, c0 : c0 + width] = residual
            squares.append(jnp.sum(residual * residual, axis=1, keepdims=True))
            outgoing = (residual * s.gain[c0 : c0 + width][None, :]).astype(BF)
        else:
            scale = lax.rsqrt(sum(squares) / D + 1e-05) + jnp.zeros((16, 128), F32)
            scale_hi = scale.astype(BF)
            scale_lo = (scale - scale_hi.astype(F32)).astype(BF)
            outgoing = jnp.where(lane < 64, scale_hi.astype(F32), scale_lo.astype(F32)).astype(
                BF
            )
        placed = jnp.dot(placing, outgoing, preferred_element_type=F32).astype(BF)
        fill(part.zs[c], placed.reshape(8, 16, width))

        @pl.loop(1, 8)
        def _(d):
            other, device = me.z_peer(d)
            send(Z, c, part.zs[c].at[other], part.zr[c].at[me.z], device)

        part.zr[c][me.z] = part.zs[c][me.z]

    def plane_out(c):
        width = WIDTHS[c]
        wait_bytes(part.zr[c].at[0:7], s.recv_sem.at[Z, c])
        rows = part.zr[c][...].reshape(128, width)
        placed = jnp.dot(to_expert, rows, preferred_element_type=F32).astype(BF)
        part.ps[c][...] = placed.reshape(8, 16, width)

        @pl.loop(1, 16)
        def _(d):
            other, device = me.plane_peer(d)
            send(
                PLANE, c, part.ps[c].at[lax.rem(other, 8)], part.xin[c].at[core, me.q], device
            )

        part.xin[c][core, me.q] = part.ps[c][lax.rem(me.q, 8)]

    def swap_out(c):
        wait_bytes(part.xin[c].at[0, 0:15], s.recv_sem.at[PLANE, c])
        mine = part.xin[c].at[core]
        swap_copies[c] = send(SWAP, c, mine, mine, me.partner)

    def hidden_units(c):
        swap_copies[c].wait_recv()
        if c == NC:
            return
        c0, width = CHUNKS[c]
        if c == 0:
            loads.gate.wait()
            loads.up.wait()
        rows = part.xin[c][...].reshape(512, WIDTHS[c])[:, 0:width]
        for weights, total in ((s.gate, s.gate_out), (s.up, s.up_out)):
            product = lax.dot_general(
                rows, weights[:, c0 : c0 + width], NT, preferred_element_type=F32
            )
            if c == 0:
                total[...] = product
            else:
                total[...] += product

    pipelined(NC + 1, (group_out, z_out, plane_out, swap_out, hidden_units), DISPATCH_TIMES)

    scales = part.xin[NC][...].reshape(512, 128).astype(F32)
    scales = scales[:, 0:1] + scales[:, 64:65]
    gate_out = s.gate_out[...] * scales
    up_out = s.up_out[...] * scales
    s.active[...] = (gate_out / (1.0 + jnp.exp(-gate_out)) * up_out).astype(BF)
    loads.down.wait()

    back_copies = {}

    def expert_out(c):
        c0, width = CHUNKS[c]
        columns = s.down[:, c0 : c0 + width]
        other_rows = s.active[pl.ds(pl.multiple_of((1 - core) * 256, 256), 256), :]
        results = jnp.dot(other_rows, columns, preferred_element_type=F32)
        fill(part.ycs[c], results.astype(BF))
        back_copies[c] = send(BC, c, part.ycs[c], part.ycr[c], me.partner)
        my_rows = s.active[pl.ds(pl.multiple_of(core * 256, 256), 256), :]
        fill(part.ymine[c], jnp.dot(my_rows, columns, preferred_element_type=F32))

    def plane_back(c):
        width = WIDTHS[c]
        back_copies[c].wait_recv()
        total = part.ymine[c][...] + part.ycr[c][...].astype(F32)
        part.ysum[c][...] = total.astype(BF).reshape(16, 16, width)

        @pl.loop(1, 16)
        def _(d):
            other, device = me.plane_peer(d)
            send(BP, c, part.ysum[c].at[other], part.pr[c].at[me.q], device)

        part.pr[c][me.q] = part.ysum[c][me.q]

    def z_back(c):
        width = WIDTHS[c]
        wait_bytes(part.pr[c].at[0:15], s.recv_sem.at[BP, c])
        rows = part.pr[c][...].reshape(256, width)
        part.vs[c][...] = (
            jnp.dot(to_source, rows, preferred_element_type=F32).astype(BF).reshape(8, 16, width)
        )

        @pl.loop(1, 8)
        def _(d):
            other, device = me.z_peer(d)
            send(BZ, c, part.vs[c].at[other], part.vr[c].at[me.z], device)

        part.vr[c][me.z] = part.vs[c][me.z]

    def finish(c):
        c0, width = CHUNKS[c]
        wait_bytes(part.vr[c].at[0:7], s.recv_sem.at[BZ, c])
        rows = part.vr[c][...].reshape(128, WIDTHS[c])[:, 0:width]
        mixed = jnp.dot(weight_hi, rows, preferred_element_type=F32) + jnp.dot(
            weight_lo, rows, preferred_element_type=F32
        )
        out[:, c0 : c0 + width] = (s.residual[:, c0 : c0 + width] + mixed).astype(BF)

    pipelined(NC, (expert_out, plane_back, z_back, finish), RETURN_TIMES)

    wait_bytes(s.proj_out.at[0:15], s.send_sem.at[PA, 0])
    wait_bytes(s.att_out.at[0:15], s.send_sem.at[AA, 0])
    for c in range(NC + 1):
        wait_bytes(part.zs[c].at[0:7], s.send_sem.at[Z, c])
        wait_bytes(part.xin[c].at[0, 0:15], s.send_sem.at[PLANE, c])
        swap_copies[c].wait_send()
    for c in range(NC):
        core_copies[c].wait_send()
        back_copies[c].wait_send()
        wait_bytes(part.rsum[c].at[0:7], s.send_sem.at[RS, c])
        wait_bytes(part.ysum[c].at[0:15], s.send_sem.at[BP, c])
        wait_bytes(part.vs[c].at[0:7], s.send_sem.at[BZ, c])


CHUNKED = dict(
    rcs=(NC, (128,), BF),
    rcr=(NC, (128,), BF),
    rmine=(NC, (128,), F32),
    rsum=(NC, (8, 16), BF),
    rrec=(NC, (8, 16), BF),
    zs=(NC + 1, (8, 16), BF),
    zr=(NC + 1, (8, 16), BF),
    ps=(NC + 1, (8, 16), BF),
    xin=(NC + 1, (2, 16, 16), BF),
    ycs=(NC, (256,), BF),
    ycr=(NC, (256,), BF),
    ymine=(NC, (256,), F32),
    ysum=(NC, (16, 16), BF),
    pr=(NC, (16, 16), BF),
    vs=(NC, (8, 16), BF),
    vr=(NC, (8, 16), BF),
)
SCRATCH = dict(
    hidden=pltpu.VMEM((D, 256), BF),
    w_in=pltpu.VMEM((160, D), BF),
    w_gain=pltpu.VMEM((160, D), BF),
    gain_in=pltpu.VMEM((D,), F32),
    keys=pltpu.VMEM((16, 128, 256), BF),
    values=pltpu.VMEM((16, 128, 256), BF),
    proj_out=pltpu.VMEM((16, 16, 256), BF),
    proj_in=pltpu.VMEM((8, 2, 16, 256), BF),
    spreading=pltpu.VMEM((320, 640), BF),
    heads=pltpu.VMEM((640, 128), F32),
    mixed=pltpu.VMEM((512, 128), F32),
    att_out=pltpu.VMEM((16, 16, 128), BF),
    att=pltpu.VMEM((8, 2, 16, 128), BF),
    own_hidden=pltpu.VMEM((16, D), F32),
    w_out=pltpu.VMEM((D, 128), BF),
    gain=pltpu.VMEM((D,), F32),
    index=pltpu.VMEM((4, 16), jnp.int32),
    share=pltpu.VMEM((4, 16), F32),
    gate=pltpu.VMEM((FFQ, D), BF),
    up=pltpu.VMEM((FFQ, D), BF),
    down=pltpu.VMEM((FFQ, D), BF),
    residual=pltpu.VMEM((16, D), F32),
    gate_out=pltpu.VMEM((512, FFQ), F32),
    up_out=pltpu.VMEM((512, FFQ), F32),
    active=pltpu.VMEM((512, FFQ), BF),
    load_sem=pltpu.SemaphoreType.DMA((12,)),
    send_sem=pltpu.SemaphoreType.DMA((10, NC + 1)),
    recv_sem=pltpu.SemaphoreType.DMA((10, NC + 1)),
)
PARTS = [
    pltpu.VMEM((*lead, WIDTHS[c]), dtype) for n, lead, dtype in CHUNKED.values() for c in range(n)
]


def per_device(
    hidden_rows,
    attention_gain,
    input_weight,
    cache_keys,
    cache_values,
    context_length,
    sink_logits,
    out_weight,
    expert_gain,
    expert_index,
    expert_share,
    gate_weight,
    up_weight,
    down_weight,
):
    scalars = pl.BlockSpec(memory_space=pltpu.SMEM)
    anywhere = pl.BlockSpec(memory_space=pltpu.HBM)
    return pl.pallas_call(
        layer,
        out_shape=jax.ShapeDtypeStruct((16, D), BF),
        in_specs=[scalars] * 2 + [anywhere] * 12,
        out_specs=pl.BlockSpec(memory_space=pltpu.VMEM),
        scratch_shapes=list(SCRATCH.values()) + PARTS,
        compiler_params=pltpu.CompilerParams(
            collective_id=0, has_side_effects=True, vmem_limit_bytes=60 * 1024 * 1024
        ),
        cost_estimate=pl.CostEstimate(
            flops=4_000_000_000, bytes_accessed=12_000_000, transcendentals=300_000
        ),
        name="layer",
    )(
        context_length,
        sink_logits,
        hidden_rows.T,
        input_weight.T,
        attention_gain,
        cache_keys,
        cache_values,
        out_weight.T,
        expert_gain,
        expert_index.T,
        expert_share.T,
        gate_weight,
        up_weight,
        down_weight,
    )


def solution(mesh):
    return jax.shard_map(
        per_device,
        mesh=mesh,
        in_specs=(
            P("attn", None),
            P(),
            P(None, "exp"),
            P(("attn", "exp"), None, None),
            P(("attn", "exp"), None, None),
            P(("attn", "exp")),
            P(),
            P("exp", None),
            P(),
            P(("attn", "exp"), None),
            P(("attn", "exp"), None),
            P(("attn", "exp"), None),
            P(("attn", "exp"), None),
            P(("attn", "exp"), None),
        ),
        out_specs=P(("attn", "exp"), None),
        check_vma=False,
    )
```

time: 430 us -> 93.9 us (0.22)
  blocking collectives: 206 us -> 0 us
  waiting for transfers between devices: 112 us -> 0 us
  Pallas kernels: 0 us -> 92.2 us
  local copies, waits for them, and re-layouts: 49 us -> 1.54 us
  matrix products: 20.4 us -> 0 us
  starting transfers between devices: 15.6 us -> 0 us
  between operations: 13.7 us -> 0.01 us
  other arithmetic: 11.2 us -> 0 us
    all_to_all x4 -> x0, blocking collectives: 206 us -> none  [the longest x1 73.9 us: per_device(): lax.all_to_all(spread_rows, 'attn', split_axis=0, concat_axis=0, tiled=True)]
    pallas_call x0 -> x1, Pallas kernels: none -> 92.2 us  [per_device(): pl.pallas_call(layer, out_shape=jax.ShapeDtypeStruct((16, D), BF), in_spe...]
    reduce_scatter x1 -> x0, waiting for transfers between devices: 69.9 us -> none  [per_device(): lax.psum_scatter(jnp.dot(attended, out_weight, preferred_element_type=jnp...]
    all_to_all x2 -> x0, waiting for transfers between devices: 41.7 us -> none  [the longest x1 38.3 us: per_device(): lax.all_to_all(lax.all_to_all(partial_value, 'attn', split_axis=0, concat...]
    dot_general x8 -> x0, matrix products: 20.4 us -> none  [the longest x1 7.15 us: expert_part(): jnp.dot(active, down_rows, preferred_element_type=jnp.float32)]
    reshape x7 -> x0, local copies, waits for them, and re-layouts: 19.6 us -> none  [the longest x1 7.14 us: expert_part(): flat_rows = rows_in.reshape(-1, rows_in.shape[-1])]
    all_to_all x2 -> x0, starting transfers between devices: 15.6 us -> none  [the longest x1 8.45 us: per_device(): lax.all_to_all(projected, 'exp', split_axis=0, concat_axis=1, tiled=True)]
    reduce_sum x6 -> x0, other arithmetic: 9.58 us -> none  [the longest x1 5.49 us: per_device(): summed = returned.astype(jnp.float32).reshape(attn_count, EXP_ATTN, quart...]
  transfers between devices with their start and end apart: 3 -> 0, of which waited for: 3 -> 0; matrix products, arithmetic and copies ran while one was open for 2% -> 0% of each run, Pallas kernels for 0% -> 0%
where the time goes in v2:
time: 93.9 us; the launch traced here: 93.8 us
  Pallas kernels  92.2 us (98%)
  local copies, waits for them, and re-layouts  1.54 us (2%)
    pallas_call x1, Pallas kernels, per_device(): pl.pallas_call(layer, out_shape=jax.ShapeDtypeStruct((16, D), BF), in_spe...  92.2 us

profile of v2, /device:TPU:1, one launch (start us, length us, event | category | flops | bytes accessed | tf_op | source)
XLA Modules:
  0.0 93.8 jit_solution(7854002920207429781)
XLA Ops:
  0.0 92.2 %layer.1 = bf16[16,2880]{1,0:T(8,128)(2,1)} custom-call(s32[16]{0:T(128)} %context.1, f32[32]{0:T(128)} %sinks.1, bf16[2880,256]{1,0:T(8,128)(2,1)} %bitcast.5, bf16[160,2880]{1,0:T(8,128)(2,1)} %bitcast.6, f32[2880]{0:T(1024)} %gain_in_hbm.1, bf16[16,128,256]{2,1,0:T(8,128)(2,1)} %keys_hbm.1, bf16[16,128,256]{2,1,0:T(8,128)(2,1)} %values_hbm.1, ...), custom_call_target="tpu_custom_call" | custom-call | flops 4000000000 | bytes 12000000 | tf_op jit(solution)/shard_map/layer/pallas_call | solution.py:579
  92.2 1.5 %copy.16 = bf16[16,2880]{1,0:T(8,128)(2,1)} copy(bf16[16,2880]{1,0:T(8,128)(2,1)} %layer.1) | data formatting | bytes 184320

commit v3 on v2

--- a/solution.py
+++ b/solution.py
@@ -12,7 +12,7 @@
 FFQ = 360
 CHUNKS = ((0, 512), (512, 512), (1024, 512), (1536, 512), (2048, 512), (2560, 320))
 NC = len(CHUNKS)
-DISPATCH_TIMES = ((0, 1), (2.1, 1), (4.2, 1), (6.3, 1), (7.4, 1))
+DISPATCH_TIMES = ((0, 1), (2.1, 1), (5.2, 1), (8.3, 1), (9.4, 1))
 RETURN_TIMES = ((0, 1), (1.1, 1), (4.2, 1), (7.3, 1))
 WIDTHS = tuple((width + 127) // 128 * 128 for _, width in CHUNKS) + (128,)
 BF = jnp.bfloat16

time: 93.9 us -> 91.6 us (0.976)
  Pallas kernels: 92.2 us -> 89.9 us
    pallas_call x1, Pallas kernels: 92.2 us -> 89.9 us  [per_device(): pl.pallas_call(layer, out_shape=jax.ShapeDtypeStruct((16, D), BF), in_spe...]
where the time goes in v3:
time: 91.6 us; the launch traced here: 91.4 us
  Pallas kernels  89.9 us (98%)
  local copies, waits for them, and re-layouts  1.54 us (2%)
    pallas_call x1, Pallas kernels, per_device(): pl.pallas_call(layer, out_shape=jax.ShapeDtypeStruct((16, D), BF), in_spe...  89.9 us

profile of v3, /device:TPU:1, one launch (start us, length us, event | category | flops | bytes accessed | tf_op | source)
XLA Modules:
  0.0 91.4 jit_solution(7351134615395706200)
XLA Ops:
  0.0 89.9 %layer.1 = bf16[16,2880]{1,0:T(8,128)(2,1)} custom-call(s32[16]{0:T(128)} %context.1, f32[32]{0:T(128)} %sinks.1, bf16[2880,256]{1,0:T(8,128)(2,1)} %bitcast.5, bf16[160,2880]{1,0:T(8,128)(2,1)} %bitcast.6, f32[2880]{0:T(1024)} %gain_in_hbm.1, bf16[16,128,256]{2,1,0:T(8,128)(2,1)} %keys_hbm.1, bf16[16,128,256]{2,1,0:T(8,128)(2,1)} %values_hbm.1, ...), custom_call_target="tpu_custom_call" | custom-call | flops 4000000000 | bytes 12000000 | tf_op jit(solution)/shard_map/layer/pallas_call | solution.py:579
  89.9 1.5 %copy.16 = bf16[16,2880]{1,0:T(8,128)(2,1)} copy(bf16[16,2880]{1,0:T(8,128)(2,1)} %layer.1) | data formatting | bytes 184320

commit v4 on v3

--- a/solution.py
+++ b/solution.py
@@ -12,8 +12,8 @@
 FFQ = 360
 CHUNKS = ((0, 512), (512, 512), (1024, 512), (1536, 512), (2048, 512), (2560, 320))
 NC = len(CHUNKS)
-DISPATCH_TIMES = ((0, 1), (2.1, 1), (5.2, 1), (8.3, 1), (9.4, 1))
-RETURN_TIMES = ((0, 1), (1.1, 1), (4.2, 1), (7.3, 1))
+DISPATCH_TIMES = ((0, 1), (2.1, 1), (5.2, 1), (9.3, 1), (10.4, 1))
+RETURN_TIMES = ((0, 1), (1.1, 1), (5.2, 1), (9.3, 1))
 WIDTHS = tuple((width + 127) // 128 * 128 for _, width in CHUNKS) + (128,)
 BF = jnp.bfloat16
 F32 = jnp.float32

time: 91.6 us -> 91.4 us (level)
  no operation moved by 1% of the time
where the time goes in v4:
time: 91.4 us; the launch traced here: 91.2 us
  Pallas kernels  89.7 us (98%)
  local copies, waits for them, and re-layouts  1.54 us (2%)
    pallas_call x1, Pallas kernels, per_device(): pl.pallas_call(layer, out_shape=jax.ShapeDtypeStruct((16, D), BF), in_spe...  89.7 us

profile of v4, /device:TPU:1, one launch (start us, length us, event | category | flops | bytes accessed | tf_op | source)
XLA Modules:
  0.0 91.2 jit_solution(15218767321128068717)
XLA Ops:
  0.0 89.7 %layer.1 = bf16[16,2880]{1,0:T(8,128)(2,1)} custom-call(s32[16]{0:T(128)} %context.1, f32[32]{0:T(128)} %sinks.1, bf16[2880,256]{1,0:T(8,128)(2,1)} %bitcast.5, bf16[160,2880]{1,0:T(8,128)(2,1)} %bitcast.6, f32[2880]{0:T(1024)} %gain_in_hbm.1, bf16[16,128,256]{2,1,0:T(8,128)(2,1)} %keys_hbm.1, bf16[16,128,256]{2,1,0:T(8,128)(2,1)} %values_hbm.1, ...), custom_call_target="tpu_custom_call" | custom-call | flops 4000000000 | bytes 12000000 | tf_op jit(solution)/shard_map/layer/pallas_call | solution.py:579
  89.7 1.5 %copy.16 = bf16[16,2880]{1,0:T(8,128)(2,1)} copy(bf16[16,2880]{1,0:T(8,128)(2,1)} %layer.1) | data formatting | bytes 184320
